TPU v7x, 32 devices: a whole 2x2x4 slice. The times are simulated.
32 devices in a mesh: groups: 2 (over x), fsdp: 16 (over z, y, core).
Axes of the slice: x: 2, y: 2, z: 4, core: 2. Of those that a mesh axis runs over, the one named last changes fastest.
Arguments:
- activations: bfloat16 [4096, 8192], P(('groups', 'fsdp')), parts along dimension 0, may hold values from -6 to 6
- grad_out: bfloat16 [4096, 1024], P(('groups', 'fsdp')), parts along dimension 0, may hold values from -1.5 to 1.5
- token_tenant: int32 [4096], P(('groups', 'fsdp')), parts along dimension 0, may hold values from -1 to 15, as said below
- segment_offsets: int32 [34], P('groups'), parts along dimension 0, may hold values from 0 to 2048, as said below
- value_weight: bfloat16 [8192, 1024], P('fsdp'), may hold values from -0.0625 to 0.0625
- down_weight_pool: bfloat16 [16, 16, 8192], P('fsdp'), may hold values from -0.0625 to 0.0625
- up_weight_pool: bfloat16 [16, 16, 1024], P('fsdp'), may hold values from -0.359375 to 0.359375
- page_table: int32 [16], replicated, may hold values from 0 to 15, each once
Outputs:
- adapted_value_output: bfloat16 [4096, 1024], P(('groups', 'fsdp')), parts along dimension 0
- input_gradient: bfloat16 [4096, 8192], P(('groups', 'fsdp')), parts along dimension 0
- down_pool_gradient: float32 [32, 16, 8192], P(('groups', 'fsdp')), parts along dimension 0
- up_pool_gradient: float32 [32, 16, 1024], P(('groups', 'fsdp')), parts along dimension 0
There are 2 independent parts, one for each index of `groups`. A program takes and returns all parts, laid end to end along the dimension named above; an argument that names none is the same for every part. Nothing has to cross between parts.
Inputs may be any that keep to these rules, and one draw needn't show every extreme that they name: `token_tenant`: rows come in aligned blocks of 128 rows; all live rows of a block belong to one tenant and the first row of every block is live. Tenant ids never fall from block to block. Padding rows (-1) stand only at the end of the last block of a tenant's segment. A tenant's segment may span several devices; some tenants have no rows. `segment_offsets`: Multiples of 128, never falling, the first 0 and the last 2048; tenant t's blocks are rows segment_offsets[t] to segment_offsets[t + 1] - 1, in agreement with token_tenant. `page_table`: each slot holds exactly one tenant's page; slot s lies on device s of fsdp.
All inputs are finite; a program needn't handle non-finite values.
Results may differ from a plain program's by a relative error of at most 0.0031.
Values may be sent and summed in bfloat16 or wider, within the bound.
A program may use at most 128 MiB of HBM per device.

v0:
```python
import jax
import jax.numpy as jnp
from jax import lax
from jax.sharding import PartitionSpec as P

BLOCK = 128


adapter_scale_factor = 2.0


def on_device(
    activations,
    grad_out,
    token_tenant,
    segment_offsets,
    value_weight,
    down_weight_pool,
    up_weight_pool,
    page_table,
):
    devices = lax.axis_size("fsdp")
    tok_rows, hidden_model_width = activations.shape
    output_width = grad_out.shape[1]
    local_slot_count = down_weight_pool.shape[0]
    adapter_rank_size = down_weight_pool.shape[1]
    tenants = page_table.shape[0]
    local_block_count = tok_rows // BLOCK
    blocks_all = local_block_count * devices
    active_token_rows = token_tenant >= 0
    masked_grad = grad_out * active_token_rows.astype(jnp.bfloat16)[:, None]
    contract_last = (((1,), (1,)), ((), ()))
    full_weight = lax.all_gather(value_weight, "fsdp", axis=0, tiled=True)
    base_output_rows = jnp.dot(activations, full_weight, preferred_element_type=jnp.float32)
    base_gradient_input = lax.dot_general(
        masked_grad, full_weight, contract_last, preferred_element_type=jnp.float32
    )
    flattened_down_weight = down_weight_pool.reshape(
        local_slot_count, adapter_rank_size * hidden_model_width
    )
    flattened_up_weight = up_weight_pool.reshape(local_slot_count, adapter_rank_size * output_width)
    held_down, held_up = (
        lax.all_to_all(flattened_down_weight, "fsdp", split_axis=1, concat_axis=0, tiled=True),
        lax.all_to_all(flattened_up_weight, "fsdp", split_axis=1, concat_axis=0, tiled=True),
    )
    share_down = held_down.shape[1]
    share_up = held_up.shape[1]
    block_first = lax.iota(jnp.int32, blocks_all) * BLOCK
    block_tenant = jnp.sum(
        (segment_offsets[1:][None, :] <= block_first[:, None]).astype(jnp.int32), axis=1
    )
    tenant_match = block_tenant[:, None] == lax.iota(jnp.int32, tenants)[None, :]
    block_slot = jnp.sum(jnp.where(tenant_match, page_table[None, :], 0), axis=1)
    send_down = jnp.take(held_down, block_slot, axis=0).reshape(
        devices, local_block_count, share_down
    )
    send_up = jnp.take(held_up, block_slot, axis=0).reshape(devices, local_block_count, share_up)
    fetched_down_weight, fetched_up_weight = (
        lax.all_to_all(send_down, "fsdp", split_axis=0, concat_axis=2, tiled=True),
        lax.all_to_all(send_up, "fsdp", split_axis=0, concat_axis=2, tiled=True),
    )
    down_weight_block = fetched_down_weight.reshape(
        local_block_count, adapter_rank_size, hidden_model_width
    )
    up_weight_block = fetched_up_weight.reshape(local_block_count, adapter_rank_size, output_width)
    input_blocks = activations.reshape(local_block_count, BLOCK, hidden_model_width)
    gradient_blocks = masked_grad.reshape(local_block_count, BLOCK, output_width)
    reduced_rank_rows = jnp.einsum(
        "bnd,brd->bnr", input_blocks, down_weight_block, preferred_element_type=jnp.float32
    ).astype(jnp.bfloat16)
    expanded_rows = jnp.einsum(
        "bnr,bro->bno", reduced_rank_rows, up_weight_block, preferred_element_type=jnp.float32
    ).reshape(tok_rows, output_width)
    pulled_rows = jnp.einsum(
        "bno,bro->bnr", gradient_blocks, up_weight_block, preferred_element_type=jnp.float32
    ).astype(jnp.bfloat16)
    scattered_gradient = jnp.einsum(
        "bnr,brd->bnd", pulled_rows, down_weight_block, preferred_element_type=jnp.float32
    ).reshape(tok_rows, hidden_model_width)
    adapted_value_output = (
        (base_output_rows + adapter_scale_factor * expanded_rows)
        * active_token_rows.astype(jnp.float32)[:, None]
    ).astype(jnp.bfloat16)
    input_gradient = (base_gradient_input + adapter_scale_factor * scattered_gradient).astype(
        jnp.bfloat16
    )
    down_weight_terms = adapter_scale_factor * jnp.einsum(
        "kpz,kpj->kzj", pulled_rows, input_blocks, preferred_element_type=jnp.float32
    )
    up_weight_terms = adapter_scale_factor * jnp.einsum(
        "yig,yiw->ygw", reduced_rank_rows, gradient_blocks, preferred_element_type=jnp.float32
    )
    ret_down = down_weight_terms.reshape(local_block_count, devices, share_down)
    ret_up = up_weight_terms.reshape(local_block_count, devices, share_up)
    back_down, back_up = (
        lax.all_to_all(ret_down, "fsdp", split_axis=1, concat_axis=0, tiled=True),
        lax.all_to_all(ret_up, "fsdp", split_axis=1, concat_axis=0, tiled=True),
    )
    recv_down = back_down.reshape(blocks_all, share_down)
    recv_up = back_up.reshape(blocks_all, share_up)
    slot_match = (block_slot[None, :] == lax.iota(jnp.int32, tenants)[:, None]).astype(jnp.float32)
    sum_down = jnp.dot(
        slot_match, recv_down, precision=lax.Precision.HIGHEST, preferred_element_type=jnp.float32
    )
    sum_up = jnp.dot(
        slot_match, recv_up, precision=lax.Precision.HIGHEST, preferred_element_type=jnp.float32
    )
    resident_down_weight, resident_up_weight = (
        lax.all_to_all(sum_down, "fsdp", split_axis=0, concat_axis=1, tiled=True),
        lax.all_to_all(sum_up, "fsdp", split_axis=0, concat_axis=1, tiled=True),
    )
    down_pool_gradient = resident_down_weight.reshape(
        local_slot_count, adapter_rank_size, hidden_model_width
    )
    up_pool_gradient = resident_up_weight.reshape(local_slot_count, adapter_rank_size, output_width)
    return (adapted_value_output, input_gradient, down_pool_gradient, up_pool_gradient)


def solution(mesh):
    placed = (
        P(("groups", "fsdp"), None),
        P(("groups", "fsdp"), None),
        P(("groups", "fsdp")),
        P("groups"),
        P("fsdp", None),
        P("fsdp", None, None),
        P("fsdp", None, None),
        P(),
    )
    return jax.shard_map(
        on_device,
        mesh=mesh,
        in_specs=placed,
        out_specs=(
            P(("groups", "fsdp"), None),
            P(("groups", "fsdp"), None),
            P(("groups", "fsdp"), None, None),
            P(("groups", "fsdp"), None, None),
        ),
        check_vma=False,
    )
```

profile of v0, /device:TPU:0, one launch (start us, length us, event | category | flops | bytes accessed | tf_op | source)
XLA Modules:
  0.0 202.2 jit_solution(9464538797833443172)
XLA Ops:
  10.7 7.4 %all-to-all-start.2 = ((bf16[16,2,512]{2,1,0:T(2,128)(2,1)}), bf16[16,2,512]{2,1,0:T(2,128)(2,1)S(1)}, u32[]{:S(2)}, u32[]{:S(2)}) async-start(bf16[16,2,512]{2,1,0:T(2,128)(2,1)} %reshape.214), calls=%async_computation.2 | async-start | bytes 65536 | tf_op jit(solution)/shard_map/all_to_all | solution.py:44
  19.9 1.5 copy.78
  21.4 2.2 %reduce = bf16[16,8192]{1,0:T(8,128)(2,1)S(1)} reduce(bf16[16,1,8192]{2,1,0:T(2,128)(2,1)S(1)} %bitcast.61, bf16[]{:T(256)} %broadcast.107), dimensions={1}, to_apply=%bitcast.55.reduce_sub_computation | reduce | bytes 524290
  24.7 5.8 %all-to-all-start = ((bf16[16,2,4096]{2,1,0:T(2,128)(2,1)}), bf16[16,2,4096]{2,1,0:T(2,128)(2,1)S(1)}, u32[]{:S(2)}, u32[]{:S(2)}) async-start(bf16[16,2,4096]{2,1,0:T(2,128)(2,1)} %reshape.210), calls=%async_computation | async-start | bytes 524288 | tf_op jit(solution)/shard_map/all_to_all | solution.py:43
  32.6 12.6 %all-to-all-done = bf16[16,2,4096]{2,1,0:T(2,128)(2,1)S(1)} async-done(((bf16[16,2,4096]{2,1,0:T(2,128)(2,1)}), bf16[16,2,4096]{2,1,0:T(2,128)(2,1)S(1)}, u32[]{:S(2)}, u32[]{:S(2)}) %all-to-all-start) | async-done | bytes 262176 | tf_op jit(solution)/shard_map/all_to_all | solution.py:43
  45.2 6.0 %all-to-all-start.3 = ((bf16[16,2,512]{2,1,0:T(2,128)(2,1)}), bf16[16,2,512]{2,1,0:T(2,128)(2,1)S(1)}, u32[]{:S(2)}, u32[]{:S(2)}) async-start(bf16[16,2,512]{2,1,0:T(2,128)(2,1)} %reshape.216), calls=%async_computation.3 | async-start | bytes 65536 | tf_op jit(solution)/shard_map/all_to_all | solution.py:60
  54.3 4.1 %all-to-all-done.3 = bf16[16,2,512]{2,1,0:T(2,128)(2,1)S(1)} async-done(((bf16[16,2,512]{2,1,0:T(2,128)(2,1)}), bf16[16,2,512]{2,1,0:T(2,128)(2,1)S(1)}, u32[]{:S(2)}, u32[]{:S(2)}) %all-to-all-start.3) | async-done | bytes 32800 | tf_op jit(solution)/shard_map/all_to_all | solution.py:60
  58.4 3.5 %all-to-all-start.1 = ((bf16[16,2,4096]{2,1,0:T(2,128)(2,1)}), bf16[16,2,4096]{2,1,0:T(2,128)(2,1)S(1)}, u32[]{:S(2)}, u32[]{:S(2)}) async-start(bf16[16,2,4096]{2,1,0:T(2,128)(2,1)} %reshape.212), calls=%async_computation.1 | async-start | bytes 524288 | tf_op jit(solution)/shard_map/all_to_all | solution.py:59
  62.8 9.2 %all-to-all-done.1 = bf16[16,2,4096]{2,1,0:T(2,128)(2,1)S(1)} async-done(((bf16[16,2,4096]{2,1,0:T(2,128)(2,1)}), bf16[16,2,4096]{2,1,0:T(2,128)(2,1)S(1)}, u32[]{:S(2)}, u32[]{:S(2)}) %all-to-all-start.1) | async-done | bytes 262176 | tf_op jit(solution)/shard_map/all_to_all | solution.py:59
  73.9 3.5 %all-to-all-start.6 = ((f32[1,16,1024]{2,0,1:T(1,128)}), f32[1,16,1024]{2,0,1:T(1,128)S(1)}, u32[]{:S(2)}, u32[]{:S(2)}) async-start(f32[1,16,1024]{2,0,1:T(1,128)} %copy.38), calls=%async_computation.6 | async-start | bytes 131072 | tf_op jit(solution)/shard_map/all_to_all | solution.py:97
  77.8 1.3 copy.36
  79.1 6.5 %all-to-all-done.6 = f32[1,16,1024]{2,0,1:T(1,128)S(1)} async-done(((f32[1,16,1024]{2,0,1:T(1,128)}), f32[1,16,1024]{2,0,1:T(1,128)S(1)}, u32[]{:S(2)}, u32[]{:S(2)}) %all-to-all-start.6) | async-done | bytes 65568 | tf_op jit(solution)/shard_map/all_to_all | solution.py:97
  85.6 3.6 %all-to-all-start.4 = ((f32[1,16,8192]{2,0,1:T(1,128)}), f32[1,16,8192]{2,0,1:T(1,128)S(1)}, u32[]{:S(2)}, u32[]{:S(2)}) async-start(f32[1,16,8192]{2,0,1:T(1,128)} %copy.36), calls=%async_computation.4 | async-start | bytes 1048576 | tf_op jit(solution)/shard_map/all_to_all | solution.py:96
  90.0 22.1 %all-to-all-done.4 = f32[1,16,8192]{2,0,1:T(1,128)S(1)} async-done(((f32[1,16,8192]{2,0,1:T(1,128)}), f32[1,16,8192]{2,0,1:T(1,128)S(1)}, u32[]{:S(2)}, u32[]{:S(2)}) %all-to-all-start.4) | async-done | bytes 524320 | tf_op jit(solution)/shard_map/all_to_all | solution.py:96
  112.2 10.5 %all-to-all-start.7 = ((f32[16,1,1024]{2,1,0:T(1,128)}), f32[16,1,1024]{2,1,0:T(1,128)S(1)}, u32[]{:S(2)}, u32[]{:S(2)}) async-start(f32[16,1,1024]{2,1,0:T(1,128)} %copy.39), calls=%async_computation.7 | async-start | bytes 131072 | tf_op jit(solution)/shard_map/all_to_all | solution.py:110
  123.4 1.3 copy.37
  124.7 6.2 %all-to-all-done.7 = f32[16,1,1024]{2,1,0:T(1,128)S(1)} async-done(((f32[16,1,1024]{2,1,0:T(1,128)}), f32[16,1,1024]{2,1,0:T(1,128)S(1)}, u32[]{:S(2)}, u32[]{:S(2)}) %all-to-all-start.7) | async-done | bytes 65568 | tf_op jit(solution)/shard_map/all_to_all | solution.py:110
  131.0 4.1 %all-to-all-start.5 = ((f32[16,1,8192]{2,1,0:T(1,128)}), f32[16,1,8192]{2,1,0:T(1,128)S(1)}, u32[]{:S(2)}, u32[]{:S(2)}) async-start(f32[16,1,8192]{2,1,0:T(1,128)} %copy.37), calls=%async_computation.5 | async-start | bytes 1048576 | tf_op jit(solution)/shard_map/all_to_all | solution.py:109
  135.7 22.4 %all-to-all-done.5 = f32[16,1,8192]{2,1,0:T(1,128)S(1)} async-done(((f32[16,1,8192]{2,1,0:T(1,128)}), f32[16,1,8192]{2,1,0:T(1,128)S(1)}, u32[]{:S(2)}, u32[]{:S(2)}) %all-to-all-start.5) | async-done | bytes 524320 | tf_op jit(solution)/shard_map/all_to_all | solution.py:109
  158.1 1.1 copy.40
  159.2 9.4 %all-gather.2.cloned.1.call-done = bf16[8192,1024]{1,0:T(8,128)(2,1)} async-done(((bf16[512,1024]{1,0:T(8,128)(2,1)}), bf16[8192,1024]{1,0:T(8,128)(2,1)}) %all-gather.2.cloned.1.call-update) | async-done | bytes 16777232 | tf_op jit(solution)/shard_map/all_gather | solution.py:33
  168.6 13.4 %fusion.13 = f32[128,8192]{1,0:T(8,128)} fusion(bf16[8192,1024]{1,0:T(8,128)(2,1)} %all-gather.2.cloned.1.call-done, bf16[128,1024]{1,0:T(8,128)(2,1)S(1)} %copy-done.1, bf16[128]{0:T(256)(128)(2,1)S(1)} %get-tuple-element.16), kind=kOutput, calls=%fused_computation.25 | convolution fusion | flops 2147614720 | bytes 21233920 | tf_op jit(solution)/shard_map/dot_general | solution.py:35
  182.0 4.2 %fusion.1 = bf16[128,8192]{1,0:T(8,128)(2,1)} fusion(f32[128,8192]{1,0:T(8,128)} %fusion.13, bf16[128,16]{0,1:T(8,128)(2,1)S(1)} %convolution_convert_fusion, bf16[16,1,8192]{2,1,0:T(2,128)(2,1)S(1)} %reshape.213), kind=kOutput, calls=%fused_computation.4 | convolution fusion | flops 36700160 | bytes 6557696 | tf_op jit(solution)/shard_map/bnr,brd->bnd/dot_general | solution.py:77
  186.2 8.1 %fusion.29 = f32[128,1024]{1,0:T(8,128)S(1)} fusion(bf16[128,8192]{1,0:T(8,128)(2,1)S(1)} %copy-done, bf16[8192,1024]{1,0:T(8,128)(2,1)} %all-gather.2.cloned.1.call-done), kind=kOutput, calls=%fused_computation.56 | convolution fusion | flops 2147483648 | bytes 19398656 | tf_op jit(solution)/shard_map/dot_general | solution.py:34
  (48 shorter events, 17.7 us)
Async XLA Ops:
  7.2 65.1 %copy-start = (bf16[128,8192]{1,0:T(8,128)(2,1)S(1)}, bf16[128,8192]{1,0:T(8,128)(2,1)}, u32[]{:S(2)}) copy-start(bf16[128,8192]{1,0:T(8,128)(2,1)} %param.8) | copy-start | bytes 6291460
  7.2 161.5 %all-gather.2.cloned.1.call-start = ((), (), s32[]{:S(2)}) async-start(), calls=%async_computation.8 | async-start | bytes 17825792 | tf_op jit(solution)/shard_map/all_gather | solution.py:33
  10.7 14.0 %all-to-all-start.2 = ((bf16[16,2,512]{2,1,0:T(2,128)(2,1)}), bf16[16,2,512]{2,1,0:T(2,128)(2,1)S(1)}, u32[]{:S(2)}, u32[]{:S(2)}) async-start(bf16[16,2,512]{2,1,0:T(2,128)(2,1)} %reshape.214), calls=%async_computation.2 | async-start | bytes 65536 | tf_op jit(solution)/shard_map/all_to_all | solution.py:44
  21.4 40.6 %copy-start.3 = (s32[128]{0:T(128)S(1)}, s32[128]{0:T(128)}, u32[]{:S(2)}) copy-start(s32[128]{0:T(128)} %param.10) | copy-start | bytes 1540
  21.4 41.2 %copy-start.1 = (bf16[128,1024]{1,0:T(8,128)(2,1)S(1)}, bf16[128,1024]{1,0:T(8,128)(2,1)}, u32[]{:S(2)}) copy-start(bf16[128,1024]{1,0:T(8,128)(2,1)} %param.9) | copy-start | bytes 786436
  24.7 20.4 %all-to-all-start = ((bf16[16,2,4096]{2,1,0:T(2,128)(2,1)}), bf16[16,2,4096]{2,1,0:T(2,128)(2,1)S(1)}, u32[]{:S(2)}, u32[]{:S(2)}) async-start(bf16[16,2,4096]{2,1,0:T(2,128)(2,1)} %reshape.210), calls=%async_computation | async-start | bytes 524288 | tf_op jit(solution)/shard_map/all_to_all | solution.py:43
  45.2 13.2 %all-to-all-start.3 = ((bf16[16,2,512]{2,1,0:T(2,128)(2,1)}), bf16[16,2,512]{2,1,0:T(2,128)(2,1)S(1)}, u32[]{:S(2)}, u32[]{:S(2)}) async-start(bf16[16,2,512]{2,1,0:T(2,128)(2,1)} %reshape.216), calls=%async_computation.3 | async-start | bytes 65536 | tf_op jit(solution)/shard_map/all_to_all | solution.py:60
  58.4 13.5 %all-to-all-start.1 = ((bf16[16,2,4096]{2,1,0:T(2,128)(2,1)}), bf16[16,2,4096]{2,1,0:T(2,128)(2,1)S(1)}, u32[]{:S(2)}, u32[]{:S(2)}) async-start(bf16[16,2,4096]{2,1,0:T(2,128)(2,1)} %reshape.212), calls=%async_computation.1 | async-start | bytes 524288 | tf_op jit(solution)/shard_map/all_to_all | solution.py:59
  73.9 11.7 %all-to-all-start.6 = ((f32[1,16,1024]{2,0,1:T(1,128)}), f32[1,16,1024]{2,0,1:T(1,128)S(1)}, u32[]{:S(2)}, u32[]{:S(2)}) async-start(f32[1,16,1024]{2,0,1:T(1,128)} %copy.38), calls=%async_computation.6 | async-start | bytes 131072 | tf_op jit(solution)/shard_map/all_to_all | solution.py:97
  85.6 26.6 %all-to-all-start.4 = ((f32[1,16,8192]{2,0,1:T(1,128)}), f32[1,16,8192]{2,0,1:T(1,128)S(1)}, u32[]{:S(2)}, u32[]{:S(2)}) async-start(f32[1,16,8192]{2,0,1:T(1,128)} %copy.36), calls=%async_computation.4 | async-start | bytes 1048576 | tf_op jit(solution)/shard_map/all_to_all | solution.py:96
  112.2 18.8 %all-to-all-start.7 = ((f32[16,1,1024]{2,1,0:T(1,128)}), f32[16,1,1024]{2,1,0:T(1,128)S(1)}, u32[]{:S(2)}, u32[]{:S(2)}) async-start(f32[16,1,1024]{2,1,0:T(1,128)} %copy.39), calls=%async_computation.7 | async-start | bytes 131072 | tf_op jit(solution)/shard_map/all_to_all | solution.py:110
  131.0 27.1 %all-to-all-start.5 = ((f32[16,1,8192]{2,1,0:T(1,128)}), f32[16,1,8192]{2,1,0:T(1,128)S(1)}, u32[]{:S(2)}, u32[]{:S(2)}) async-start(f32[16,1,8192]{2,1,0:T(1,128)} %copy.37), calls=%async_computation.5 | async-start | bytes 1048576 | tf_op jit(solution)/shard_map/all_to_all | solution.py:109
  186.2 8.1 %copy-start.2 = (f32[128]{0:T(128)S(1)}, f32[128]{0:T(128)}, u32[]{:S(2)}) copy-start(f32[128]{0:T(128)} %get-tuple-element.17) | copy-start | bytes 1540
Sparse Core Ops, SparseCore 0:
  10.2 158.4 all-gather.1
where the time goes:
time: 203 us; the launch traced here: 202 us
  waiting for transfers between devices  93.5 us (46%)
  starting transfers between devices  44.5 us (22%)
  matrix products  29 us (14%)
  local copies, waits for them, and re-layouts  14.6 us (7%)
  between operations  14.3 us (7%)
  other arithmetic  6.27 us (3%)
    all_to_all x1, waiting for transfers between devices, on_device(): lax.all_to_all(sum_down, 'fsdp', split_axis=0, concat_axis=1, tiled=True)  22.4 us
    all_to_all x1, waiting for transfers between devices, on_device(): lax.all_to_all(ret_down, 'fsdp', split_axis=1, concat_axis=0, tiled=True)  22.1 us
    dot_general x1, matrix products, on_device(): lax.dot_general(masked_grad, full_weight, contract_last, preferred_elemen...  13.4 us
    all_to_all x1, waiting for transfers between devices, on_device(): lax.all_to_all(flattened_down_weight, 'fsdp', split_axis=1, concat_axis=0...  12.6 us
    all_to_all x1, starting transfers between devices, on_device(): lax.all_to_all(sum_up, 'fsdp', split_axis=0, concat_axis=1, tiled=True)  10.5 us
    all_gather x1, waiting for transfers between devices, on_device(): full_weight = lax.all_gather(value_weight, 'fsdp', axis=0, tiled=True)  9.43 us
    all_to_all x1, waiting for transfers between devices, on_device(): lax.all_to_all(send_down, 'fsdp', split_axis=0, concat_axis=2, tiled=True)  9.18 us
    unnamed x23, local copies, waits for them, and re-layouts  8.53 us
  transfers between devices with their start and end apart: 9, of which 9 were waited for; matrix products, arithmetic and copies ran while one was open for 11% of the time, Pallas kernels for 0%

commit v1 on v0

--- a/solution.py
+++ b/solution.py
@@ -1,6 +1,10 @@
+import functools
+
 import jax
 import jax.numpy as jnp
 from jax import lax
+from jax.experimental import pallas as pl
+from jax.experimental.pallas import tpu as pltpu
 from jax.sharding import PartitionSpec as P
 
 BLOCK = 128
@@ -116,6 +120,415 @@
     return (adapted_value_output, input_gradient, down_pool_gradient, up_pool_gradient)
 
 
+LAST = (((1,), (1,)), ((), ()))
+FIRST = (((0,), (0,)), ((), ()))
+LANES = 128
+
+
+def remote(src, dst, send, recv, where):
+    return pltpu.make_async_remote_copy(
+        src_ref=src,
+        dst_ref=dst,
+        send_sem=send,
+        recv_sem=recv,
+        device_id=where,
+        device_id_type=pl.DeviceIdType.MESH,
+    )
+
+
+def fused_kernel(
+    n,
+    acts,
+    grad,
+    tenant,
+    offsets,
+    table,
+    w_hbm,
+    down,
+    up,
+    out,
+    ig,
+    down_grad,
+    up_grad,
+    w_all,
+    mg,
+    total,
+    share_out,
+    share_in0,
+    share_in1,
+    share_in2,
+    share_in3,
+    slots,
+    pulled2,
+    live_col,
+    local_sem,
+    ring_send,
+    ring_recv,
+    x_send,
+    x_recv,
+    core_send,
+    core_recv,
+    corex_send,
+    corex_recv,
+    own_send,
+    own_recv,
+    share_send,
+    share_recv,
+):
+    share_in = (share_in0, share_in1, share_in2, share_in3)
+    x = lax.axis_index("groups")
+    f = lax.axis_index("fsdp")
+    m = n // 2
+    half = m // 2
+    chip, core = lax.div(f, 2), lax.rem(f, 2)
+    z, y = lax.div(chip, 2), lax.rem(chip, 2)
+    p = z + y * (m - 1 - 2 * z)
+    width = down.shape[2] // n
+    out_width = up.shape[2]
+    ups = out_width // LANES
+    rows = w_all.shape[1]
+    cut = ((rows * 176) // 512) // 16 * 16
+    length = rows - cut
+    first = (length // 2 + 15) // 16 * 16
+
+    def chip_at(position):
+        q = lax.rem(position + 2 * m, m)
+        y_q = lax.div(q, half)
+        return 2 * (q + y_q * (m - 1 - 2 * q)) + y_q
+
+    def at(shard, start, size):
+        return w_all.at[shard, pl.ds(pl.multiple_of(start, 16), size), :]
+
+    right = {"fsdp": 2 * chip_at(p + 1) + core}
+    left = {"fsdp": 2 * chip_at(p - 1) + core}
+    sibling = {"fsdp": 2 * chip + 1 - core}
+    across = {"groups": 1 - x}
+    ring_start = x * cut
+    mine_start = x * length
+    other_start = (1 - x) * length
+
+    barrier = pltpu.get_barrier_semaphore()
+
+    @pl.loop(1, n)
+    def _(d):
+        pl.semaphore_signal(
+            barrier,
+            inc=1,
+            device_id={"fsdp": lax.rem(f + d, n)},
+            device_id_type=pl.DeviceIdType.MESH,
+        )
+
+    pl.semaphore_signal(barrier, inc=1, device_id=across, device_id_type=pl.DeviceIdType.MESH)
+    load = pltpu.make_async_copy(w_hbm, w_all.at[f], local_sem)
+    load.start()
+    for j in range(n):
+        share_out[0, j, :, :width] = down[0, :, j * width : (j + 1) * width]
+        k = j % ups
+        share_out[0, j, :, width:] = up[0, :, k * LANES : (k + 1) * LANES]
+    pl.semaphore_wait(barrier, n)
+
+    def share_copy(phase, j, slot):
+        return remote(
+            share_out.at[phase, j],
+            share_in[phase].at[slot],
+            share_send.at[phase, j],
+            share_recv.at[phase, slot],
+            {"fsdp": j},
+        )
+
+    def share_start(phase):
+        @pl.loop(1, n)
+        def _(d):
+            j = lax.rem(f + d, n)
+            share_copy(phase, j, f).start()
+
+        share_in[phase][f] = share_out[phase, f]
+
+    def share_wait(phase):
+        @pl.loop(1, n)
+        def _(d):
+            j = lax.rem(f + d, n)
+            share_copy(phase, j, j).wait_recv()
+
+    sends = []
+
+    def go(copy):
+        copy.start()
+        sends.append(copy)
+
+    def ring_copy(way, s, shard):
+        if s < half:
+            start, size = ring_start, length
+        elif way == 0:
+            start, size = ring_start, first
+        else:
+            start, size = ring_start + first, length - first
+        part = at(shard, start, size)
+        return remote(
+            part,
+            part,
+            ring_send.at[way, s - 1],
+            ring_recv.at[way, s - 1],
+            (right, left)[way],
+        )
+
+    def x_copy(way, s, shard, start):
+        part = at(shard, start, cut)
+        return remote(part, part, x_send.at[way, s - 1], x_recv.at[way, s - 1], across)
+
+    def core_copy(way, s, shard):
+        part = at(shard, ring_start, length)
+        return remote(part, part, core_send.at[way, s - 1], core_recv.at[way, s - 1], sibling)
+
+    def corex_copy(way, s, shard):
+        part = at(shard, other_start, cut)
+        return remote(part, part, corex_send.at[way, s - 1], corex_recv.at[way, s - 1], sibling)
+
+    def shard_of(way, s, c):
+        return 2 * chip_at(p - s if way == 0 else p + s) + c
+
+    def pass_on(s):
+        for way in range(2):
+            shard = shard_of(way, s, core)
+            ring_copy(way, s, shard).wait_recv()
+            if s < half:
+                go(ring_copy(way, s + 1, shard))
+                go(x_copy(way, s, shard, mine_start))
+                go(core_copy(way, s, shard))
+        if s == half:
+            shard = shard_of(0, s, core)
+            go(x_copy(0, s, shard, mine_start))
+            go(core_copy(0, s, shard))
+
+    def finish(s):
+        ways = 2 if s < half else 1
+        for way in range(ways):
+            shard = shard_of(way, s, core)
+            x_copy(way, s, shard, other_start).wait_recv()
+            go(corex_copy(way, s, shard))
+        for way in range(ways):
+            shard = shard_of(way, s, 1 - core)
+            core_copy(way, s, shard).wait_recv()
+            corex_copy(way, s, shard).wait_recv()
+
+    def consume(shard):
+        columns = pl.ds(pl.multiple_of(shard * width, LANES), width)
+        w = w_all[shard]
+        total[...] += jnp.dot(acts[:, columns], w, preferred_element_type=jnp.float32)
+        back = lax.dot_general(mg[...], w, LAST, preferred_element_type=jnp.float32)
+        back += jnp.dot(
+            pulled2[...], share_in1[shard, :, :width], preferred_element_type=jnp.float32
+        )
+        ig[:, columns] = back.astype(jnp.bfloat16)
+
+    def compute(s):
+        count = 4 if 0 < s < half else 2
+
+        @pl.loop(0, count)
+        def _(t):
+            sign = 2 * lax.div(t, 2) - 1
+            consume(2 * chip_at(p + s * sign) + lax.rem(t, 2))
+
+    share_start(0)
+    load.wait()
+    for way in range(2):
+        go(ring_copy(way, 1, f))
+    own = remote(w_all.at[f], w_all.at[f], own_send, own_recv, sibling)
+    go(own)
+
+    live = (tenant[...] >= 0).astype(jnp.float32)
+    size = live.shape[1]
+    diagonal = lax.broadcasted_iota(jnp.int32, (size, size), 0) == lax.broadcasted_iota(
+        jnp.int32, (size, size), 1
+    )
+    live_col[...] = jnp.sum(
+        jnp.where(diagonal, jnp.broadcast_to(live, (size, size)), 0.0), axis=1, keepdims=True
+    )
+    mg[...] = (grad[...].astype(jnp.float32) * live_col[...]).astype(jnp.bfloat16)
+    tenants = table.shape[0]
+
+    @pl.loop(0, n)
+    def _(b):
+        tenant_of = lax.fori_loop(
+            0,
+            tenants,
+            lambda t, count: count + (offsets[t + 1] <= b * BLOCK).astype(jnp.int32),
+            jnp.int32(0),
+        )
+        slots[b] = table[jnp.minimum(tenant_of, tenants - 1)]
+
+    share_wait(0)
+
+    @pl.loop(0, n)
+    def _(b):
+        share_out[1, b] = share_in0[slots[b]]
+
+    share_start(1)
+    pass_on(1)
+    share_wait(1)
+
+    rank = down.shape[1]
+    shrunk = jnp.zeros((rank, size), jnp.float32)
+    pulled = jnp.zeros((rank, size), jnp.float32)
+    for j in range(n):
+        shrunk += lax.dot_general(
+            share_in1[j, :, :width],
+            acts[:, j * width : (j + 1) * width],
+            LAST,
+            preferred_element_type=jnp.float32,
+        )
+    for k in range(ups):
+        pulled += lax.dot_general(
+            share_in1[k, :, width:],
+            mg[:, k * LANES : (k + 1) * LANES],
+            LAST,
+            preferred_element_type=jnp.float32,
+        )
+    scale = adapter_scale_factor
+    shrunk2_f32 = shrunk.astype(jnp.bfloat16).astype(jnp.float32) * scale
+    pulled2_f32 = pulled.astype(jnp.bfloat16).astype(jnp.float32) * scale
+    shrunk2_t = shrunk2_f32.astype(jnp.bfloat16)
+    pulled2_t = pulled2_f32.astype(jnp.bfloat16)
+    shrunk2 = shrunk2_f32.T.astype(jnp.bfloat16)
+    pulled2[...] = pulled2_f32.T.astype(jnp.bfloat16)
+    for j in range(n):
+        share_out[2, j, :, :width] = jnp.dot(
+            pulled2_t, acts[:, j * width : (j + 1) * width], preferred_element_type=jnp.float32
+        ).astype(jnp.bfloat16)
+    for k in range(ups):
+        columns = slice(k * LANES, (k + 1) * LANES)
+        term = jnp.dot(shrunk2_t, mg[:, columns], preferred_element_type=jnp.float32).astype(
+            jnp.bfloat16
+        )
+        for j in range(k, n, ups):
+            share_out[2, j, :, width:] = term
+        total[:, columns] = jnp.dot(
+            shrunk2, share_in1[k, :, width:], preferred_element_type=jnp.float32
+        )
+    share_start(2)
+    remote(
+        w_all.at[2 * chip + 1 - core], w_all.at[2 * chip + 1 - core], own_send, own_recv, sibling
+    ).wait_recv()
+    compute(0)
+    for s in range(2, half + 1):
+        pass_on(s)
+        if s == 2:
+            share_wait(2)
+
+            @pl.loop(0, n)
+            def _(slot):
+                summed = jnp.zeros(share_in2.shape[1:], jnp.float32)
+                for b in range(n):
+                    summed += jnp.where(
+                        slots[b] == slot, share_in2[b].astype(jnp.float32), 0.0
+                    )
+                share_out[3, slot] = summed.astype(jnp.bfloat16)
+
+            share_start(3)
+        finish(s - 1)
+        compute(s - 1)
+    share_wait(3)
+    for j in range(n):
+        down_grad[0, :, j * width : (j + 1) * width] = share_in3[j, :, :width].astype(jnp.float32)
+    for k in range(ups):
+        up_grad[0, :, k * LANES : (k + 1) * LANES] = share_in3[k, :, width:].astype(jnp.float32)
+    finish(half)
+    compute(half)
+    out[...] = (total[...] * live_col[...]).astype(jnp.bfloat16)
+    for copy in sends:
+        copy.wait_send()
+    for phase in range(4):
+
+        @pl.loop(1, n)
+        def _(d):
+            share_copy(phase, lax.rem(f + d, n), f).wait_send()
+
+
+def fused(
+    activations,
+    grad_out,
+    token_tenant,
+    segment_offsets,
+    value_weight,
+    down_weight_pool,
+    up_weight_pool,
+    page_table,
+):
+    n = lax.axis_size("fsdp")
+    tokens, model = activations.shape
+    rows, out_width = value_weight.shape
+    rank = down_weight_pool.shape[1]
+    steps = n // 4
+    vmem = pl.BlockSpec(memory_space=pltpu.VMEM)
+    smem = pl.BlockSpec(memory_space=pltpu.SMEM)
+    dma = pltpu.SemaphoreType.DMA
+    return pl.pallas_call(
+        functools.partial(fused_kernel, n),
+        out_shape=(
+            jax.ShapeDtypeStruct((tokens, out_width), jnp.bfloat16),
+            jax.ShapeDtypeStruct((tokens, model), jnp.bfloat16),
+            jax.ShapeDtypeStruct((1, rank, model), jnp.float32),
+            jax.ShapeDtypeStruct((1, rank, out_width), jnp.float32),
+        ),
+        in_specs=[vmem, vmem, vmem, smem, smem, pl.BlockSpec(memory_space=pl.ANY), vmem, vmem],
+        out_specs=[vmem] * 4,
+        scratch_shapes=[
+            pltpu.VMEM((n, rows, out_width), jnp.bfloat16),
+            pltpu.VMEM((tokens, out_width), jnp.bfloat16),
+            pltpu.VMEM((tokens, out_width), jnp.float32),
+            pltpu.VMEM((4, n, rank, model // n + LANES), jnp.bfloat16),
+            pltpu.VMEM((n, rank, model // n + LANES), jnp.bfloat16),
+            pltpu.VMEM((n, rank, model // n + LANES), jnp.bfloat16),
+            pltpu.VMEM((n, rank, model // n + LANES), jnp.bfloat16),
+            pltpu.VMEM((n, rank, model // n + LANES), jnp.bfloat16),
+            pltpu.SMEM((n,), jnp.int32),
+            pltpu.VMEM((tokens, rank), jnp.bfloat16),
+            pltpu.VMEM((tokens, 1), jnp.float32),
+            dma,
+        ]
+        + [dma((2, steps))] * 8
+        + [dma, dma, dma((4, n)), dma((4, n))],
+        compiler_params=pltpu.CompilerParams(
+            collective_id=0, has_side_effects=True, vmem_limit_bytes=56 * 2**20
+        ),
+        cost_estimate=pl.CostEstimate(
+            flops=4 * tokens * model * out_width,
+            bytes_accessed=4 * tokens * model + 4 * model * out_width // n,
+            transcendentals=0,
+        ),
+    )(
+        activations,
+        grad_out,
+        token_tenant.reshape(1, tokens),
+        segment_offsets,
+        page_table,
+        value_weight,
+        down_weight_pool,
+        up_weight_pool,
+    )
+
+
+def either(*args):
+    n = lax.axis_size("fsdp")
+    tokens, model = args[0].shape
+    rows, out_width = args[4].shape
+    slots, rank = args[5].shape[:2]
+    fits = (
+        lax.axis_size("groups") == 2
+        and n % 8 == 0
+        and n <= 32
+        and tokens == BLOCK
+        and slots == 1
+        and rank % 16 == 0
+        and model % (n * LANES) == 0
+        and out_width % LANES == 0
+        and out_width // LANES <= n
+        and rows >= 128
+        and rows % 16 == 0
+    )
+    return (fused if fits else on_device)(*args)
+
+
 def solution(mesh):
     placed = (
         P(("groups", "fsdp"), None),
@@ -128,7 +541,7 @@
         P(),
     )
     return jax.shard_map(
-        on_device,
+        either,
         mesh=mesh,
         in_specs=placed,
         out_specs=(

time: 203 us -> 116 us (0.57)
  the two profiles are of different devices: /device:TPU:0 before, /device:TPU:17 now
where the time goes in v1:
time: 116 us; the launch traced here: 115 us
  Pallas kernels  108 us (93%)
  local copies, waits for them, and re-layouts  6.26 us (5%)
    pallas_call x1, Pallas kernels, fused(): pl.pallas_call(functools.partial(fused_kernel, n), out_shape=(jax.ShapeDt...  108 us
    unnamed x8, local copies, waits for them, and re-layouts  6.26 us

profile of v1, /device:TPU:17, one launch (start us, length us, event | category | flops | bytes accessed | tf_op | source)
XLA Modules:
  0.0 115.3 jit_solution(10022713835283020817)
XLA Ops:
  0.6 108.4 %shard_map.111 = (bf16[128,1024]{1,0:T(8,128)(2,1)}, bf16[128,8192]{1,0:T(8,128)(2,1)}, f32[1,16,8192]{2,1,0:T(8,128)}, f32[1,16,1024]{2,1,0:T(8,128)}) custom-call(bf16[128,8192]{1,0:T(8,128)(2,1)} %acts.1, bf16[128,1024]{1,0:T(8,128)(2,1)} %grad.1, s32[1,128]{1,0:T(1,128)} %bitcast.1, s32[17]{0:T(128)} %offsets.1, s32[16]{0:T(128)} %table.1, ...), custom_call_target="tpu_custom_call" | custom-call | flops 4294967296 | bytes 6291456 | tf_op jit(solution)/shard_map/pallas_call | solution.py:465
  109.0 1.7 %copy.16 = bf16[128,1024]{1,0:T(8,128)(2,1)} copy(bf16[128,1024]{1,0:T(8,128)(2,1)} %get-tuple-element.8) | data formatting | bytes 524288
  110.7 0.0 copy-start
  110.7 0.0 copy-start.1
  110.7 3.2 %copy.17 = bf16[128,8192]{1,0:T(8,128)(2,1)} copy(bf16[128,8192]{1,0:T(8,128)(2,1)} %get-tuple-element.9) | data formatting | bytes 4194304
  113.9 0.0 copy-done
  113.9 0.8 copy.18
  114.7 0.0 copy-done.1
  114.7 0.6 copy.19
Async XLA Ops:
  110.7 3.2 %copy-start = (f32[1,16,8192]{2,1,0:T(8,128)S(1)}, f32[1,16,8192]{2,1,0:T(8,128)}, u32[]{:S(2)}) copy-start(f32[1,16,8192]{2,1,0:T(8,128)} %get-tuple-element.10) | copy-start | bytes 1572868
  110.7 4.0 %copy-start.1 = (f32[1,16,1024]{2,1,0:T(8,128)S(1)}, f32[1,16,1024]{2,1,0:T(8,128)}, u32[]{:S(2)}) copy-start(f32[1,16,1024]{2,1,0:T(8,128)} %get-tuple-element.11) | copy-start | bytes 196612

commit v2 on v1

--- a/solution.py
+++ b/solution.py
@@ -189,7 +189,6 @@
     rows = w_all.shape[1]
     cut = ((rows * 176) // 512) // 16 * 16
     length = rows - cut
-    first = (length // 2 + 15) // 16 * 16
 
     def chip_at(position):
         q = lax.rem(position + 2 * m, m)
@@ -203,7 +202,6 @@
     left = {"fsdp": 2 * chip_at(p - 1) + core}
     sibling = {"fsdp": 2 * chip + 1 - core}
     across = {"groups": 1 - x}
-    ring_start = x * cut
     mine_start = x * length
     other_start = (1 - x) * length
 
@@ -256,19 +254,16 @@
         copy.start()
         sends.append(copy)
 
-    def ring_copy(way, s, shard):
-        if s < half:
-            start, size = ring_start, length
-        elif way == 0:
-            start, size = ring_start, first
+    def ring_copy(way, s, piece, shard):
+        if piece == 0:
+            part = at(shard, mine_start, cut)
         else:
-            start, size = ring_start + first, length - first
-        part = at(shard, start, size)
+            part = at(shard, cut, length - cut)
         return remote(
             part,
             part,
-            ring_send.at[way, s - 1],
-            ring_recv.at[way, s - 1],
+            ring_send.at[way, s - 1, piece],
+            ring_recv.at[way, s - 1, piece],
             (right, left)[way],
         )
 
@@ -276,9 +271,18 @@
         part = at(shard, start, cut)
         return remote(part, part, x_send.at[way, s - 1], x_recv.at[way, s - 1], across)
 
-    def core_copy(way, s, shard):
-        part = at(shard, ring_start, length)
-        return remote(part, part, core_send.at[way, s - 1], core_recv.at[way, s - 1], sibling)
+    def core_copy(way, s, piece, shard):
+        if piece == 0:
+            part = at(shard, mine_start, cut)
+        else:
+            part = at(shard, cut, length - cut)
+        return remote(
+            part,
+            part,
+            core_send.at[way, s - 1, piece],
+            core_recv.at[way, s - 1, piece],
+            sibling,
+        )
 
     def corex_copy(way, s, shard):
         part = at(shard, other_start, cut)
@@ -287,18 +291,16 @@
     def shard_of(way, s, c):
         return 2 * chip_at(p - s if way == 0 else p + s) + c
 
-    def pass_on(s):
-        for way in range(2):
+    def pass_on(s, piece):
+        for way in range(2) if s < half else (piece,):
             shard = shard_of(way, s, core)
-            ring_copy(way, s, shard).wait_recv()
-            if s < half:
-                go(ring_copy(way, s + 1, shard))
-                go(x_copy(way, s, shard, mine_start))
-                go(core_copy(way, s, shard))
-        if s == half:
-            shard = shard_of(0, s, core)
-            go(x_copy(0, s, shard, mine_start))
-            go(core_copy(0, s, shard))
+            ring_copy(way, s, piece, shard).wait_recv()
+            if s + 1 < half or (s + 1 == half and way == piece):
+                go(ring_copy(way, s + 1, piece, shard))
+            slot = way if s < half else 0
+            if piece == 0:
+                go(x_copy(slot, s, shard, mine_start))
+            go(core_copy(slot, s, piece, shard))
 
     def finish(s):
         ways = 2 if s < half else 1
@@ -308,7 +310,8 @@
             go(corex_copy(way, s, shard))
         for way in range(ways):
             shard = shard_of(way, s, 1 - core)
-            core_copy(way, s, shard).wait_recv()
+            for piece in range(2):
+                core_copy(way, s, piece, shard).wait_recv()
             corex_copy(way, s, shard).wait_recv()
 
     def consume(shard):
@@ -331,8 +334,9 @@
 
     share_start(0)
     load.wait()
-    for way in range(2):
-        go(ring_copy(way, 1, f))
+    for piece in range(2):
+        for way in range(2):
+            go(ring_copy(way, 1, piece, f))
     own = remote(w_all.at[f], w_all.at[f], own_send, own_recv, sibling)
     go(own)
 
@@ -357,6 +361,8 @@
         )
         slots[b] = table[jnp.minimum(tenant_of, tenants - 1)]
 
+    pass_on(1, 0)
+    pass_on(1, 1)
     share_wait(0)
 
     @pl.loop(0, n)
@@ -364,7 +370,8 @@
         share_out[1, b] = share_in0[slots[b]]
 
     share_start(1)
-    pass_on(1)
+    pass_on(2, 0)
+    pass_on(2, 1)
     share_wait(1)
 
     rank = down.shape[1]
@@ -410,23 +417,27 @@
         w_all.at[2 * chip + 1 - core], w_all.at[2 * chip + 1 - core], own_send, own_recv, sibling
     ).wait_recv()
     compute(0)
-    for s in range(2, half + 1):
-        pass_on(s)
-        if s == 2:
-            share_wait(2)
-
-            @pl.loop(0, n)
-            def _(slot):
-                summed = jnp.zeros(share_in2.shape[1:], jnp.float32)
-                for b in range(n):
-                    summed += jnp.where(
-                        slots[b] == slot, share_in2[b].astype(jnp.float32), 0.0
-                    )
-                share_out[3, slot] = summed.astype(jnp.bfloat16)
-
-            share_start(3)
-        finish(s - 1)
-        compute(s - 1)
+    finish(1)
+    compute(1)
+    pass_on(3, 0)
+    pass_on(3, 1)
+    share_wait(2)
+
+    @pl.loop(0, n)
+    def _(slot):
+        summed = jnp.zeros(share_in2.shape[1:], jnp.float32)
+        for b in range(n):
+            summed += jnp.where(slots[b] == slot, share_in2[b].astype(jnp.float32), 0.0)
+        share_out[3, slot] = summed.astype(jnp.bfloat16)
+
+    share_start(3)
+    finish(2)
+    compute(2)
+    for s in range(3, half):
+        pass_on(s + 1, 0)
+        pass_on(s + 1, 1)
+        finish(s)
+        compute(s)
     share_wait(3)
     for j in range(n):
         down_grad[0, :, j * width : (j + 1) * width] = share_in3[j, :, :width].astype(jnp.float32)
@@ -486,7 +497,10 @@
             pltpu.VMEM((tokens, 1), jnp.float32),
             dma,
         ]
-        + [dma((2, steps))] * 8
+        + [dma((2, steps, 2))] * 2
+        + [dma((2, steps))] * 2
+        + [dma((2, steps, 2))] * 2
+        + [dma((2, steps))] * 2
         + [dma, dma, dma((4, n)), dma((4, n))],
         compiler_params=pltpu.CompilerParams(
             collective_id=0, has_side_effects=True, vmem_limit_bytes=56 * 2**20

time: 116 us -> 108 us (0.931)
  Pallas kernels: 108 us -> 101 us
    pallas_call x1, Pallas kernels: 108 us -> 101 us  [fused(): pl.pallas_call(functools.partial(fused_kernel, n), out_shape=(jax.ShapeDt...]
where the time goes in v2:
time: 108 us
  Pallas kernels  101 us (94%)
  local copies, waits for them, and re-layouts  6.26 us (6%)
    pallas_call x1, Pallas kernels, fused(): pl.pallas_call(functools.partial(fused_kernel, n), out_shape=(jax.ShapeDt...  101 us
    unnamed x8, local copies, waits for them, and re-layouts  6.26 us

profile of v2, /device:TPU:17, one launch (start us, length us, event | category | flops | bytes accessed | tf_op | source)
XLA Modules:
  0.0 107.9 jit_solution(2002278174359240550)
XLA Ops:
  0.6 101.0 %shard_map.111 = (bf16[128,1024]{1,0:T(8,128)(2,1)}, bf16[128,8192]{1,0:T(8,128)(2,1)}, f32[1,16,8192]{2,1,0:T(8,128)}, f32[1,16,1024]{2,1,0:T(8,128)}) custom-call(bf16[128,8192]{1,0:T(8,128)(2,1)} %acts.1, bf16[128,1024]{1,0:T(8,128)(2,1)} %grad.1, s32[1,128]{1,0:T(1,128)} %bitcast.1, s32[17]{0:T(128)} %offsets.1, s32[16]{0:T(128)} %table.1, ...), custom_call_target="tpu_custom_call" | custom-call | flops 4294967296 | bytes 6291456 | tf_op jit(solution)/shard_map/pallas_call | solution.py:476
  101.6 1.7 %copy.16 = bf16[128,1024]{1,0:T(8,128)(2,1)} copy(bf16[128,1024]{1,0:T(8,128)(2,1)} %get-tuple-element.8) | data formatting | bytes 524288
  103.3 0.0 copy-start
  103.3 0.0 copy-start.1
  103.3 3.2 %copy.17 = bf16[128,8192]{1,0:T(8,128)(2,1)} copy(bf16[128,8192]{1,0:T(8,128)(2,1)} %get-tuple-element.9) | data formatting | bytes 4194304
  106.4 0.0 copy-done
  106.4 0.8 copy.18
  107.2 0.0 copy-done.1
  107.2 0.6 copy.19
Async XLA Ops:
  103.3 3.2 %copy-start = (f32[1,16,8192]{2,1,0:T(8,128)S(1)}, f32[1,16,8192]{2,1,0:T(8,128)}, u32[]{:S(2)}) copy-start(f32[1,16,8192]{2,1,0:T(8,128)} %get-tuple-element.10) | copy-start | bytes 1572868
  103.3 4.0 %copy-start.1 = (f32[1,16,1024]{2,1,0:T(8,128)S(1)}, f32[1,16,1024]{2,1,0:T(8,128)}, u32[]{:S(2)}) copy-start(f32[1,16,1024]{2,1,0:T(8,128)} %get-tuple-element.11) | copy-start | bytes 196612

commit v3 on v2

--- a/solution.py
+++ b/solution.py
@@ -138,7 +138,7 @@
 
 def fused_kernel(
     n,
-    acts,
+    acts_hbm,
     grad,
     tenant,
     offsets,
@@ -147,7 +147,7 @@
     down,
     up,
     out,
-    ig,
+    ig_hbm,
     down_grad,
     up_grad,
     w_all,
@@ -161,6 +161,10 @@
     slots,
     pulled2,
     live_col,
+    acts,
+    ig,
+    acts_sem,
+    ig_sem,
     local_sem,
     ring_send,
     ring_recv,
@@ -187,7 +191,7 @@
     out_width = up.shape[2]
     ups = out_width // LANES
     rows = w_all.shape[1]
-    cut = ((rows * 176) // 512) // 16 * 16
+    cut = ((rows * 208) // 512) // 16 * 16
     length = rows - cut
 
     def chip_at(position):
@@ -217,8 +221,10 @@
         )
 
     pl.semaphore_signal(barrier, inc=1, device_id=across, device_id_type=pl.DeviceIdType.MESH)
+    fetch = pltpu.make_async_copy(acts_hbm, acts, acts_sem)
     load = pltpu.make_async_copy(w_hbm, w_all.at[f], local_sem)
     load.start()
+    fetch.start()
     for j in range(n):
         share_out[0, j, :, :width] = down[0, :, j * width : (j + 1) * width]
         k = j % ups
@@ -303,16 +309,21 @@
             go(core_copy(slot, s, piece, shard))
 
     def finish(s):
-        ways = 2 if s < half else 1
-        for way in range(ways):
+        for way in range(2 if s < half else 1):
             shard = shard_of(way, s, core)
             x_copy(way, s, shard, other_start).wait_recv()
             go(corex_copy(way, s, shard))
-        for way in range(ways):
+
+    def collect(s):
+        for way in range(2 if s < half else 1):
             shard = shard_of(way, s, 1 - core)
             for piece in range(2):
                 core_copy(way, s, piece, shard).wait_recv()
             corex_copy(way, s, shard).wait_recv()
+
+    def store(shard):
+        columns = pl.ds(pl.multiple_of(shard * width, LANES), width)
+        return pltpu.make_async_copy(ig.at[:, columns], ig_hbm.at[:, columns], ig_sem.at[shard])
 
     def consume(shard):
         columns = pl.ds(pl.multiple_of(shard * width, LANES), width)
@@ -323,8 +334,11 @@
             pulled2[...], share_in1[shard, :, :width], preferred_element_type=jnp.float32
         )
         ig[:, columns] = back.astype(jnp.bfloat16)
+        store(shard).start()
 
     def compute(s):
+        if s > 0:
+            collect(s)
         count = 4 if 0 < s < half else 2
 
         @pl.loop(0, count)
@@ -374,6 +388,7 @@
     pass_on(2, 1)
     share_wait(1)
 
+    fetch.wait()
     rank = down.shape[1]
     shrunk = jnp.zeros((rank, size), jnp.float32)
     pulled = jnp.zeros((rank, size), jnp.float32)
@@ -438,14 +453,18 @@
         pass_on(s + 1, 1)
         finish(s)
         compute(s)
+    finish(half)
     share_wait(3)
     for j in range(n):
         down_grad[0, :, j * width : (j + 1) * width] = share_in3[j, :, :width].astype(jnp.float32)
     for k in range(ups):
         up_grad[0, :, k * LANES : (k + 1) * LANES] = share_in3[k, :, width:].astype(jnp.float32)
-    finish(half)
     compute(half)
     out[...] = (total[...] * live_col[...]).astype(jnp.bfloat16)
+    @pl.loop(0, n)
+    def _(shard):
+        store(shard).wait()
+
     for copy in sends:
         copy.wait_send()
     for phase in range(4):
@@ -471,6 +490,7 @@
     rank = down_weight_pool.shape[1]
     steps = n // 4
     vmem = pl.BlockSpec(memory_space=pltpu.VMEM)
+    hbm = pl.BlockSpec(memory_space=pl.ANY)
     smem = pl.BlockSpec(memory_space=pltpu.SMEM)
     dma = pltpu.SemaphoreType.DMA
     return pl.pallas_call(
@@ -481,8 +501,8 @@
             jax.ShapeDtypeStruct((1, rank, model), jnp.float32),
             jax.ShapeDtypeStruct((1, rank, out_width), jnp.float32),
         ),
-        in_specs=[vmem, vmem, vmem, smem, smem, pl.BlockSpec(memory_space=pl.ANY), vmem, vmem],
-        out_specs=[vmem] * 4,
+        in_specs=[hbm, vmem, vmem, smem, smem, hbm, vmem, vmem],
+        out_specs=[vmem, hbm, vmem, vmem],
         scratch_shapes=[
             pltpu.VMEM((n, rows, out_width), jnp.bfloat16),
             pltpu.VMEM((tokens, out_width), jnp.bfloat16),
@@ -495,6 +515,10 @@
             pltpu.SMEM((n,), jnp.int32),
             pltpu.VMEM((tokens, rank), jnp.bfloat16),
             pltpu.VMEM((tokens, 1), jnp.float32),
+            pltpu.VMEM((tokens, model), jnp.bfloat16),
+            pltpu.VMEM((tokens, model), jnp.bfloat16),
+            dma,
+            dma((n,)),
             dma,
         ]
         + [dma((2, steps, 2))] * 2

time: 108 us -> 106 us (0.981)
  Pallas kernels: 101 us -> 99 us
    pallas_call x1, Pallas kernels: 101 us -> 99 us  [fused(): pl.pallas_call(functools.partial(fused_kernel, n), out_shape=(jax.ShapeDt...]
where the time goes in v3:
time: 106 us
  Pallas kernels  99 us (93%)
  local copies, waits for them, and re-layouts  6.26 us (6%)
    pallas_call x1, Pallas kernels, fused(): pl.pallas_call(functools.partial(fused_kernel, n), out_shape=(jax.ShapeDt...  99 us
    unnamed x8, local copies, waits for them, and re-layouts  6.26 us

profile of v3, /device:TPU:17, one launch (start us, length us, event | category | flops | bytes accessed | tf_op | source)
XLA Modules:
  0.0 105.9 jit_solution(2469700208692122622)
XLA Ops:
  0.6 99.0 %shard_map.111 = (bf16[128,1024]{1,0:T(8,128)(2,1)}, bf16[128,8192]{1,0:T(8,128)(2,1)}, f32[1,16,8192]{2,1,0:T(8,128)}, f32[1,16,1024]{2,1,0:T(8,128)}) custom-call(bf16[128,8192]{1,0:T(8,128)(2,1)} %acts_hbm.1, bf16[128,1024]{1,0:T(8,128)(2,1)} %grad.1, s32[1,128]{1,0:T(1,128)} %bitcast.1, s32[17]{0:T(128)} %offsets.1, s32[16]{0:T(128)} %table.1, ...), custom_call_target="tpu_custom_call" | custom-call | flops 4294967296 | bytes 6291456 | tf_op jit(solution)/shard_map/pallas_call | solution.py:496
  99.6 1.7 %copy.16 = bf16[128,1024]{1,0:T(8,128)(2,1)} copy(bf16[128,1024]{1,0:T(8,128)(2,1)} %get-tuple-element.8) | data formatting | bytes 524288
  101.3 0.0 copy-start
  101.3 0.0 copy-start.1
  101.3 3.2 %copy.17 = bf16[128,8192]{1,0:T(8,128)(2,1)} copy(bf16[128,8192]{1,0:T(8,128)(2,1)} %get-tuple-element.9) | data formatting | bytes 4194304
  104.5 0.0 copy-done
  104.5 0.8 copy.18
  105.3 0.0 copy-done.1
  105.3 0.6 copy.19
Async XLA Ops:
  101.3 3.2 %copy-start = (f32[1,16,8192]{2,1,0:T(8,128)S(1)}, f32[1,16,8192]{2,1,0:T(8,128)}, u32[]{:S(2)}) copy-start(f32[1,16,8192]{2,1,0:T(8,128)} %get-tuple-element.10) | copy-start | bytes 1572868
  101.3 4.0 %copy-start.1 = (f32[1,16,1024]{2,1,0:T(8,128)S(1)}, f32[1,16,1024]{2,1,0:T(8,128)}, u32[]{:S(2)}) copy-start(f32[1,16,1024]{2,1,0:T(8,128)} %get-tuple-element.11) | copy-start | bytes 196612

commit v4 on v3

--- a/solution.py
+++ b/solution.py
@@ -301,11 +301,11 @@
         for way in range(2) if s < half else (piece,):
             shard = shard_of(way, s, core)
             ring_copy(way, s, piece, shard).wait_recv()
-            if s + 1 < half or (s + 1 == half and way == piece):
-                go(ring_copy(way, s + 1, piece, shard))
             slot = way if s < half else 0
             if piece == 0:
                 go(x_copy(slot, s, shard, mine_start))
+            if s + 1 < half or (s + 1 == half and way == piece):
+                go(ring_copy(way, s + 1, piece, shard))
             go(core_copy(slot, s, piece, shard))
 
     def finish(s):

time: 106 us -> 106 us (level)
  no operation moved by 1% of the time
where the time goes in v4:
time: 106 us
  Pallas kernels  99 us (93%)
  local copies, waits for them, and re-layouts  6.26 us (6%)
    pallas_call x1, Pallas kernels, fused(): pl.pallas_call(functools.partial(fused_kernel, n), out_shape=(jax.ShapeDt...  99 us
    unnamed x8, local copies, waits for them, and re-layouts  6.26 us

profile of v4, /device:TPU:17, one launch (start us, length us, event | category | flops | bytes accessed | tf_op | source)
XLA Modules:
  0.0 105.9 jit_solution(7199861639350231512)
XLA Ops:
  0.6 99.0 %shard_map.111 = (bf16[128,1024]{1,0:T(8,128)(2,1)}, bf16[128,8192]{1,0:T(8,128)(2,1)}, f32[1,16,8192]{2,1,0:T(8,128)}, f32[1,16,1024]{2,1,0:T(8,128)}) custom-call(bf16[128,8192]{1,0:T(8,128)(2,1)} %acts_hbm.1, bf16[128,1024]{1,0:T(8,128)(2,1)} %grad.1, s32[1,128]{1,0:T(1,128)} %bitcast.1, s32[17]{0:T(128)} %offsets.1, s32[16]{0:T(128)} %table.1, ...), custom_call_target="tpu_custom_call" | custom-call | flops 4294967296 | bytes 6291456 | tf_op jit(solution)/shard_map/pallas_call | solution.py:496
  99.6 1.7 %copy.16 = bf16[128,1024]{1,0:T(8,128)(2,1)} copy(bf16[128,1024]{1,0:T(8,128)(2,1)} %get-tuple-element.8) | data formatting | bytes 524288
  101.3 0.0 copy-start
  101.3 0.0 copy-start.1
  101.3 3.2 %copy.17 = bf16[128,8192]{1,0:T(8,128)(2,1)} copy(bf16[128,8192]{1,0:T(8,128)(2,1)} %get-tuple-element.9) | data formatting | bytes 4194304
  104.5 0.0 copy-done
  104.5 0.8 copy.18
  105.3 0.0 copy-done.1
  105.3 0.6 copy.19
Async XLA Ops:
  101.3 3.2 %copy-start = (f32[1,16,8192]{2,1,0:T(8,128)S(1)}, f32[1,16,8192]{2,1,0:T(8,128)}, u32[]{:S(2)}) copy-start(f32[1,16,8192]{2,1,0:T(8,128)} %get-tuple-element.10) | copy-start | bytes 1572868
  101.3 4.0 %copy-start.1 = (f32[1,16,1024]{2,1,0:T(8,128)S(1)}, f32[1,16,1024]{2,1,0:T(8,128)}, u32[]{:S(2)}) copy-start(f32[1,16,1024]{2,1,0:T(8,128)} %get-tuple-element.11) | copy-start | bytes 196612

commit v5 on v4

--- a/solution.py
+++ b/solution.py
@@ -231,20 +231,29 @@
         share_out[0, j, :, width:] = up[0, :, k * LANES : (k + 1) * LANES]
     pl.semaphore_wait(barrier, n)
 
-    def share_copy(phase, j, slot):
+    def share_copy(phase, j, slot, columns):
         return remote(
-            share_out.at[phase, j],
-            share_in[phase].at[slot],
+            share_out.at[phase, j, :, pl.ds(0, columns)],
+            share_in[phase].at[slot, :, pl.ds(0, columns)],
             share_send.at[phase, j],
             share_recv.at[phase, slot],
             {"fsdp": j},
         )
+
+    def share_each(phase, j, slot, holder, act):
+        @pl.when(holder < ups)
+        def _():
+            act(share_copy(phase, j, slot, width + LANES))
+
+        @pl.when(holder >= ups)
+        def _():
+            act(share_copy(phase, j, slot, width))
 
     def share_start(phase):
         @pl.loop(1, n)
         def _(d):
             j = lax.rem(f + d, n)
-            share_copy(phase, j, f).start()
+            share_each(phase, j, f, (j, f)[phase % 2], lambda copy: copy.start())
 
         share_in[phase][f] = share_out[phase, f]
 
@@ -252,7 +261,7 @@
         @pl.loop(1, n)
         def _(d):
             j = lax.rem(f + d, n)
-            share_copy(phase, j, j).wait_recv()
+            share_each(phase, j, j, (f, j)[phase % 2], lambda copy: copy.wait_recv())
 
     sends = []
 
@@ -471,7 +480,8 @@
 
         @pl.loop(1, n)
         def _(d):
-            share_copy(phase, lax.rem(f + d, n), f).wait_send()
+            j = lax.rem(f + d, n)
+            share_each(phase, j, f, (j, f)[phase % 2], lambda copy: copy.wait_send())
 
 
 def fused(

time: 106 us -> 104 us (0.981)
  Pallas kernels: 99 us -> 96.2 us
    pallas_call x1, Pallas kernels: 99 us -> 96.2 us  [fused(): pl.pallas_call(functools.partial(fused_kernel, n), out_shape=(jax.ShapeDt...]
where the time goes in v5:
time: 104 us; the launch traced here: 103 us
  Pallas kernels  96.2 us (92%)
  local copies, waits for them, and re-layouts  6.26 us (6%)
    pallas_call x1, Pallas kernels, fused(): pl.pallas_call(functools.partial(fused_kernel, n), out_shape=(jax.ShapeDt...  96.2 us
    unnamed x8, local copies, waits for them, and re-layouts  6.26 us

profile of v5, /device:TPU:17, one launch (start us, length us, event | category | flops | bytes accessed | tf_op | source)
XLA Modules:
  0.0 103.1 jit_solution(9398981828848138696)
XLA Ops:
  0.6 96.2 %shard_map.111 = (bf16[128,1024]{1,0:T(8,128)(2,1)}, bf16[128,8192]{1,0:T(8,128)(2,1)}, f32[1,16,8192]{2,1,0:T(8,128)}, f32[1,16,1024]{2,1,0:T(8,128)}) custom-call(bf16[128,8192]{1,0:T(8,128)(2,1)} %acts_hbm.1, bf16[128,1024]{1,0:T(8,128)(2,1)} %grad.1, s32[1,128]{1,0:T(1,128)} %bitcast.1, s32[17]{0:T(128)} %offsets.1, s32[16]{0:T(128)} %table.1, ...), custom_call_target="tpu_custom_call" | custom-call | flops 4294967296 | bytes 6291456 | tf_op jit(solution)/shard_map/pallas_call | solution.py:506
  96.9 1.7 %copy.16 = bf16[128,1024]{1,0:T(8,128)(2,1)} copy(bf16[128,1024]{1,0:T(8,128)(2,1)} %get-tuple-element.8) | data formatting | bytes 524288
  98.5 0.0 copy-start
  98.5 0.0 copy-start.1
  98.5 3.2 %copy.17 = bf16[128,8192]{1,0:T(8,128)(2,1)} copy(bf16[128,8192]{1,0:T(8,128)(2,1)} %get-tuple-element.9) | data formatting | bytes 4194304
  101.7 0.0 copy-done
  101.7 0.8 copy.18
  102.5 0.0 copy-done.1
  102.5 0.6 copy.19
Async XLA Ops:
  98.5 3.2 %copy-start = (f32[1,16,8192]{2,1,0:T(8,128)S(1)}, f32[1,16,8192]{2,1,0:T(8,128)}, u32[]{:S(2)}) copy-start(f32[1,16,8192]{2,1,0:T(8,128)} %get-tuple-element.10) | copy-start | bytes 1572868
  98.5 4.0 %copy-start.1 = (f32[1,16,1024]{2,1,0:T(8,128)S(1)}, f32[1,16,1024]{2,1,0:T(8,128)}, u32[]{:S(2)}) copy-start(f32[1,16,1024]{2,1,0:T(8,128)} %get-tuple-element.11) | copy-start | bytes 196612
